TPU v7x, 32 devices: a whole 2x2x4 slice. The times are simulated.
32 devices in a mesh: day: 4 (over y, x), lon: 8 (over z, core).
Axes of the slice: x: 2, y: 2, z: 4, core: 2. Of those that a mesh axis runs over, the one named last changes fastest.
Arguments:
- observed: bfloat16 [512, 32, 1024], P('day', None, 'lon'), may hold values from -6 to 6
- decay_rate: float32 [32, 1024], P(None, 'lon'), may hold values from 0.000546875 to 0.077
- drain_factor: float32 [512, 32], P('day'), may hold values from 0.5 to 1
- smoothing: float32 [32, 1024], P(None, 'lon'), may hold values from 0.12 to 0.245
- land_mask: int32 [32, 1024], P(None, 'lon'), may hold values 0 or 1
- zone_ids: int32 [32, 8], P(('day', 'lon')), may hold values from 0 to 7
- kernels: bfloat16 [8, 512, 512], replicated, may hold values from -0.25 to 0.25
Outputs:
- zone_series: bfloat16 [512, 32, 1024], P(None, ('day', 'lon'))
All inputs are finite; a program needn't handle non-finite values. No bound on the sum of `land_mask` on one device may be relied on, other than what follows from the above.
Results may differ from a plain program's by a relative error of at most 0.0049.
Values may be sent and summed in bfloat16 or wider, within the bound.
A program may use at most 192 MiB of HBM per device.

v0:
```python
import functools

import jax
import jax.numpy as jnp
from jax import lax
from jax.experimental import pallas as pl
from jax.experimental.pallas import tpu as pltpu
from jax.sharding import PartitionSpec as P

MESH = pl.DeviceIdType.MESH
F32 = jnp.float32
RING = 4


def remote(src, dst, send, recv, device):
    return pltpu.make_async_remote_copy(
        src_ref=src, dst_ref=dst, send_sem=send, recv_sem=recv,
        device_id=device, device_id_type=MESH,
    )


def series_kernel(
    nd, nl,
    obs, decay, drain, smoothing, land, gathered,
    drain_t, drain_cum, nat, local, summary, summary_in, summary_t, strip_in,
    params_t, halo_out, halo_in, gain_self, gain_side, fade, carry_t, rings, blocks,
    sum_send, sum_recv, strip_send, strip_recv, par_send, par_recv,
    halo_send, halo_recv, row_send, row_recv, own_sem,
):
    days, rows, cells = obs.shape
    count = nd * nl
    me_d, me_l = lax.axis_index("day"), lax.axis_index("lon")
    me = me_d * nl + me_l
    east, west = lax.rem(me_l + 1, nl), lax.rem(me_l + nl - 1, nl)
    barrier = pltpu.get_barrier_semaphore()

    @pl.loop(1, count)
    def _(k):
        other = lax.rem(me + k, count)
        pl.semaphore_signal(
            barrier, inc=1, device_id=(other // nl, lax.rem(other, nl)), device_id_type=MESH
        )

    def turned(plane):
        if rows < 128:
            plane = jnp.concatenate([plane, jnp.zeros((128 - rows, cells), F32)], axis=0)
        return plane.T

    land_f = land[...].astype(F32)
    params_t[0, 8:136, :] = turned(decay[...])
    params_t[1, 8:136, :] = turned(land_f * (1.0 - 4.0 * smoothing[...]))
    params_t[2, 8:136, :] = turned(land_f * smoothing[...])
    drain_t[...] = drain[...].T
    lane = lax.broadcasted_iota(jnp.int32, (rows, days), 1)
    cum = drain_t[...]
    step = 1
    while step < days:
        cum = cum * jnp.where(lane >= step, pltpu.roll(cum, step, 1), 1.0)
        step *= 2
    drain_cum[...] = cum

    part = min(rows, 32)

    @pl.loop(0, rows // part)
    def _(b):
        band = pl.ds(pl.multiple_of(b * part, part), part)
        persist = jnp.exp(-decay[band, :])
        inject = jnp.sqrt(1.0 - persist * persist) * land[band, :].astype(F32)

        def chunk(c, level):
            factors = pltpu.roll(drain_t[band, :], lax.rem(days - 8 * c, days), 1)
            for k in range(8):
                keep = persist * factors[:, k : k + 1]
                level = keep * level + inject * obs[8 * c + k, band, :].astype(F32)
                start = pl.multiple_of((8 * c + k) * rows + b * part, part)
                nat[pl.ds(start, part), :] = level
            return level

        level = lax.fori_loop(0, days // 8, chunk, jnp.zeros((part, cells), F32))
        summary[1, band, :] = level
        summary[0, band, :] = jnp.exp(-float(days) * decay[band, :]) * drain_cum[band, days - 1 : days]

    summary_t[0] = turned(summary[0])
    summary_t[1] = turned(summary[1])

    pl.semaphore_wait(barrier, count - 1)

    copies = []
    for k in range(1, nd):
        there = lax.rem(me_d + k, nd)
        copies.append(remote(summary, summary_in.at[k], sum_send.at[k], sum_recv.at[k], (there, me_l)))
        copies.append(remote(summary_t.at[:, 120:128, :], strip_in.at[0, k], strip_send.at[0, k], strip_recv.at[0, k], (there, east)))
        copies.append(remote(summary_t.at[:, 0:8, :], strip_in.at[1, k], strip_send.at[1, k], strip_recv.at[1, k], (there, west)))
    copies.append(remote(params_t.at[:, 128:136, :], params_t.at[:, 0:8, :], par_send.at[0], par_recv.at[0], (me_d, east)))
    copies.append(remote(params_t.at[:, 8:16, :], params_t.at[:, 136:144, :], par_send.at[1], par_recv.at[1], (me_d, west)))
    for copy in copies:
        copy.start()

    @pl.loop(0, rows // 2)
    def _(i):
        first = nat[pl.ds(2 * i, days, stride=rows), :].T
        second = nat[pl.ds(2 * i + 1, days, stride=rows), :].T
        local[2 * i] = first
        local[2 * i + 1] = second
        halo_out[0, i] = jnp.concatenate([first[124:128], second[124:128]], axis=0)
        halo_out[1, i] = jnp.concatenate([first[0:4], second[0:4]], axis=0)

    copies.append(remote(halo_out.at[0], halo_in.at[0], halo_send.at[0], halo_recv.at[0], (me_d, east)))
    copies.append(remote(halo_out.at[1], halo_in.at[1], halo_send.at[1], halo_recv.at[1], (me_d, west)))
    copies[-2].start()
    copies[-1].start()

    def column(table, r):
        return pltpu.roll(table, lax.rem(128 - r, 128), 1)[:, 0:1]

    def spread(table, r):
        return jnp.broadcast_to(column(table, r), (table.shape[0], 128))

    ages = -(lax.broadcasted_iota(jnp.int32, (1, 128), 1) + 1).astype(F32)

    def faded(table, r):
        return jnp.exp(spread(table, r) * ages) * drain_cum[pl.ds(r, 1), :]

    @pl.loop(0, rows)
    def _(r):
        gain_self[r, 8:136, :] = spread(params_t[1, 8:136, :], r)
        gain_side[r, 8:136, :] = spread(params_t[2, 8:136, :], r)
        fade[r] = faded(params_t[0, 8:136, :], r)

    rings[...] = jnp.zeros_like(rings)

    for copy in copies:
        copy.wait()

    carry = jnp.zeros((rows, cells), F32)
    carry_w = jnp.zeros((8, 128), F32)
    carry_e = jnp.zeros((8, 128), F32)
    for k in range(nd - 1, 0, -1):
        used = k <= me_d
        carry = jnp.where(used, summary_in[k, 0] * carry + summary_in[k, 1], carry)
        carry_w = jnp.where(used, strip_in[0, k, 0] * carry_w + strip_in[0, k, 1], carry_w)
        carry_e = jnp.where(used, strip_in[1, k, 0] * carry_e + strip_in[1, k, 1], carry_e)
    carry_t[0:8, :] = carry_w
    carry_t[8:136, :] = turned(carry)
    carry_t[136:144, :] = carry_e

    def smooth(p, j):
        above, here, below = (
            lax.rem(jnp.maximum(j - 1, 0), RING),
            lax.rem(j, RING),
            lax.rem(jnp.minimum(j + 1, rows - 1), RING),
        )
        around = (
            rings[p - 1, here, 9:153, :] + rings[p - 1, here, 7:151, :]
            + rings[p - 1, above, 8:152, :] + rings[p - 1, below, 8:152, :]
        )
        return gain_self[j] * rings[p - 1, here, 8:152, :] + gain_side[j] * around

    @pl.loop(0, rows + 4)
    def _(i):
        @pl.when(i < rows)
        def _():
            slot = lax.rem(i, RING)
            odd = lax.rem(i, 2) == 1
            enter = spread(carry_t[...], i)
            rings[0, slot, 16:144, :] = local[i] + fade[i] * enter[8:136]
            low, high = halo_in[0, i // 2], halo_in[1, i // 2]
            low = jnp.where(odd, low, pltpu.roll(low, 4, 0))
            high = jnp.where(odd, pltpu.roll(high, 4, 0), high)
            rings[0, slot, 8:16, :] = low + faded(params_t[0, 0:8, :], i) * enter[0:8]
            rings[0, slot, 144:152, :] = high + faded(params_t[0, 136:144, :], i) * enter[136:144]
            gain_self[i, 0:8, :] = spread(params_t[1, 0:8, :], i)
            gain_self[i, 136:144, :] = spread(params_t[1, 136:144, :], i)
            gain_side[i, 0:8, :] = spread(params_t[2, 0:8, :], i)
            gain_side[i, 136:144, :] = spread(params_t[2, 136:144, :], i)

        for p in range(1, 5):
            j = i - p

            @pl.when(jnp.logical_and(j >= 0, j < rows))
            def _():
                new = smooth(p, j)
                if p < 4:
                    rings[p, lax.rem(j, RING), 8:152, :] = new
                else:
                    blocks[j] = new[8:136].astype(jnp.bfloat16)

    spot = gathered.at[me_l, :, pl.ds(pl.multiple_of(me_d * days, days), days)]

    def row_copy(k):
        other = lax.rem(me + k, count)
        return remote(
            blocks.at[other], spot, row_send.at[k], row_recv.at[k],
            (other // nl, lax.rem(other, nl)),
        )

    @pl.loop(1, count)
    def _(k):
        row_copy(k).start()

    mine = pltpu.make_async_copy(blocks.at[me], spot, own_sem)
    mine.start()
    mine.wait()

    @pl.loop(1, count)
    def _(k):
        row_copy(k).wait()


def zone_kernel(zone_ids, kernel, block, out):
    out[...] = lax.dot_general(
        kernel[0], block[0], (((1,), (1,)), ((), ())), preferred_element_type=F32
    ).astype(out.dtype)


def body(nd, nl, observed, decay_rate, drain_factor, smoothing, land_mask, zone_ids, kernels):
    days, rows, cells = observed.shape
    count = nd * nl
    total = kernels.shape[1]
    assert days == 128 and cells == 128 and rows == count
    vmem = pl.BlockSpec(memory_space=pltpu.VMEM)
    dma = pltpu.SemaphoreType.DMA
    gathered = pl.pallas_call(
        functools.partial(series_kernel, nd, nl),
        out_shape=jax.ShapeDtypeStruct((nl, cells, total), jnp.bfloat16),
        in_specs=[vmem] * 5,
        out_specs=pl.BlockSpec(memory_space=pl.ANY),
        scratch_shapes=[
            pltpu.VMEM((rows, days), F32),
            pltpu.VMEM((rows, days), F32),
            pltpu.VMEM((days * rows, cells), F32),
            pltpu.VMEM((rows, cells, days), F32),
            pltpu.VMEM((2, rows, cells), F32),
            pltpu.VMEM((nd, 2, rows, cells), F32),
            pltpu.VMEM((2, cells, 128), F32),
            pltpu.VMEM((2, nd, 2, 8, 128), F32),
            pltpu.VMEM((3, 144, 128), F32),
            pltpu.VMEM((2, rows // 2, 8, days), F32),
            pltpu.VMEM((2, rows // 2, 8, days), F32),
            pltpu.VMEM((rows, 144, 128), F32),
            pltpu.VMEM((rows, 144, 128), F32),
            pltpu.VMEM((rows, 128, 128), F32),
            pltpu.VMEM((144, 128), F32),
            pltpu.VMEM((4, RING, 160, 128), F32),
            pltpu.VMEM((rows, cells, days), jnp.bfloat16),
            dma((nd,)), dma((nd,)),
            dma((2, nd)), dma((2, nd)),
            dma((2,)), dma((2,)),
            dma((2,)), dma((2,)),
            dma((count,)), dma((count,)),
            dma,
        ],
        compiler_params=pltpu.CompilerParams(
            collective_id=0, has_side_effects=True, vmem_limit_bytes=60 * 2**20
        ),
        name="series",
    )(observed, decay_rate, drain_factor, smoothing, land_mask)
    out = pl.pallas_call(
        zone_kernel,
        out_shape=jax.ShapeDtypeStruct((total, nl * cells), jnp.bfloat16),
        grid_spec=pltpu.PrefetchScalarGridSpec(
            num_scalar_prefetch=1,
            grid=(nl,),
            in_specs=[
                pl.BlockSpec((1, total, total), lambda k, zones: (zones[0, k], 0, 0)),
                pl.BlockSpec((1, cells, total), lambda k, zones: (k, 0, 0)),
            ],
            out_specs=pl.BlockSpec((total, cells), lambda k, zones: (0, k)),
        ),
        compiler_params=pltpu.CompilerParams(vmem_limit_bytes=32 * 2**20),
        name="zones",
    )(zone_ids, kernels, gathered)
    return out.reshape(total, 1, nl * cells)


def solution(mesh):
    placed = (
        P("day", None, "lon"),
        P(None, "lon"),
        P("day", None),
        P(None, "lon"),
        P(None, "lon"),
        P(("day", "lon"), None),
        P(),
    )
    return jax.shard_map(
        functools.partial(body, mesh.shape["day"], mesh.shape["lon"]),
        mesh=mesh, in_specs=placed, out_specs=P(None, ("day", "lon"), None), check_vma=False,
    )
```

profile of v0, /device:TPU:0, one launch (start us, length us, event | category | flops | bytes accessed | tf_op | source)
XLA Modules:
  0.0 63.7 jit_solution(11540396679595523904)
XLA Ops:
  0.0 1.4 %copy.8.drain = f32[128,32]{1,0:T(8,128)} copy(f32[128,32]{0,1:T(8,128)} %param.9) | data formatting | bytes 32768 | tf_op args[2]
  1.4 53.5 %series.1.block = bf16[8,128,512]{2,1,0:T(8,128)(2,1)} custom-call(bf16[128,32,128]{2,1,0:T(8,128)(2,1)} %obs.1, f32[32,128]{1,0:T(8,128)} %decay.1, f32[128,32]{1,0:T(8,128)} %copy.8.drain, f32[32,128]{1,0:T(8,128)} %smoothing.1, s32[32,128]{1,0:T(8,128)} %land.1), custom_call_target="tpu_custom_call" | custom-call | tf_op jit(solution)/shard_map/series/pallas_call | solution.py:223
  54.9 0.0 copy-start
  54.9 1.2 %copy-done = bf16[8,128,512]{2,1,0:T(8,128)(2,1)S(1)} copy-done((bf16[8,128,512]{2,1,0:T(8,128)(2,1)S(1)}, bf16[8,128,512]{2,1,0:T(8,128)(2,1)}, u32[]{:S(2)}) %copy-start) | copy-done | bytes 1048600
  56.2 0.0 copy-start.1
  56.2 2.2 %copy-done.1 = bf16[8,512,512]{2,1,0:T(8,128)(2,1)S(1)} copy-done((bf16[8,512,512]{2,1,0:T(8,128)(2,1)S(1)}, bf16[8,512,512]{2,1,0:T(8,128)(2,1)}, u32[]{:S(2)}) %copy-start.1) | copy-done | bytes 4194328
  58.3 0.0 copy-start.2
  58.3 0.7 %copy-done.2 = s32[1,8]{1,0:T(1,128)S(1)} copy-done((s32[1,8]{1,0:T(1,128)S(1)}, s32[1,8]{1,0:T(1,128)}, u32[]{:S(2)}) %copy-start.2) | copy-done | bytes 56
  59.0 4.7 %zones.1 = bf16[512,1024]{1,0:T(8,128)(2,1)} custom-call(s32[1,8]{1,0:T(1,128)S(1)} %copy-done.2, bf16[8,512,512]{2,1,0:T(8,128)(2,1)S(1)} %copy-done.1, bf16[8,128,512]{2,1,0:T(8,128)(2,1)S(1)} %copy-done), custom_call_target="tpu_custom_call" | custom-call | tf_op jit(solution)/shard_map/zones/pallas_call | solution.py:258
Async XLA Ops:
  54.9 1.2 %copy-start = (bf16[8,128,512]{2,1,0:T(8,128)(2,1)S(1)}, bf16[8,128,512]{2,1,0:T(8,128)(2,1)}, u32[]{:S(2)}) copy-start(bf16[8,128,512]{2,1,0:T(8,128)(2,1)} %series.1.block) | copy-start | bytes 3145732
  56.2 2.2 %copy-start.1 = (bf16[8,512,512]{2,1,0:T(8,128)(2,1)S(1)}, bf16[8,512,512]{2,1,0:T(8,128)(2,1)}, u32[]{:S(2)}) copy-start(bf16[8,512,512]{2,1,0:T(8,128)(2,1)} %kernel.1) | copy-start | bytes 12582916
  58.3 0.7 %copy-start.2 = (s32[1,8]{1,0:T(1,128)S(1)}, s32[1,8]{1,0:T(1,128)}, u32[]{:S(2)}) copy-start(s32[1,8]{1,0:T(1,128)} %zone_ids.1) | copy-start | bytes 100
where the time goes:
time: 63.9 us; the launch traced here: 63.7 us
  Pallas kernels  58.1 us (91%)
  local copies, waits for them, and re-layouts  5.51 us (9%)
    pallas_call x1, Pallas kernels, body(): pl.pallas_call(functools.partial(series_kernel, nd, nl), out_shape=jax.Sh...  53.5 us
    unnamed x7, local copies, waits for them, and re-layouts  5.51 us
    pallas_call x1, Pallas kernels, body(): pl.pallas_call(zone_kernel, out_shape=jax.ShapeDtypeStruct((total, nl * c...  4.67 us

commit v1 on v0

--- a/solution.py
+++ b/solution.py
@@ -21,17 +21,21 @@
 
 def series_kernel(
     nd, nl,
-    obs, decay, drain, smoothing, land, gathered,
-    drain_t, drain_cum, nat, local, summary, summary_in, summary_t, strip_in,
-    params_t, halo_out, halo_in, gain_self, gain_side, fade, carry_t, rings, blocks,
+    zones, obs, decay, drain, smoothing, land, kernels, out,
+    drain_cum, nat, local, summary, summary_in, summary_t, strip_in,
+    params_t, halo_out, halo_in, gain_self, gain_side, carry_t, rings, blocks,
+    kernels_in, gathered, result,
     sum_send, sum_recv, strip_send, strip_recv, par_send, par_recv,
-    halo_send, halo_recv, row_send, row_recv, own_sem,
+    halo_send, halo_recv, row_send, row_recv, own_sem, kernels_sem, out_sem,
 ):
     days, rows, cells = obs.shape
     count = nd * nl
     me_d, me_l = lax.axis_index("day"), lax.axis_index("lon")
     me = me_d * nl + me_l
     east, west = lax.rem(me_l + 1, nl), lax.rem(me_l + nl - 1, nl)
+    fetch = pltpu.make_async_copy(kernels, kernels_in, kernels_sem)
+    fetch.start()
+    kept = gain_self.shape[0]
     barrier = pltpu.get_barrier_semaphore()
 
     @pl.loop(1, count)
@@ -50,9 +54,8 @@
     params_t[0, 8:136, :] = turned(decay[...])
     params_t[1, 8:136, :] = turned(land_f * (1.0 - 4.0 * smoothing[...]))
     params_t[2, 8:136, :] = turned(land_f * smoothing[...])
-    drain_t[...] = drain[...].T
     lane = lax.broadcasted_iota(jnp.int32, (rows, days), 1)
-    cum = drain_t[...]
+    cum = drain[...]
     step = 1
     while step < days:
         cum = cum * jnp.where(lane >= step, pltpu.roll(cum, step, 1), 1.0)
@@ -68,7 +71,7 @@
         inject = jnp.sqrt(1.0 - persist * persist) * land[band, :].astype(F32)
 
         def chunk(c, level):
-            factors = pltpu.roll(drain_t[band, :], lax.rem(days - 8 * c, days), 1)
+            factors = pltpu.roll(drain[band, :], lax.rem(days - 8 * c, days), 1)
             for k in range(8):
                 keep = persist * factors[:, k : k + 1]
                 level = keep * level + inject * obs[8 * c + k, band, :].astype(F32)
@@ -121,11 +124,20 @@
     def faded(table, r):
         return jnp.exp(spread(table, r) * ages) * drain_cum[pl.ds(r, 1), :]
 
-    @pl.loop(0, rows)
-    def _(r):
-        gain_self[r, 8:136, :] = spread(params_t[1, 8:136, :], r)
-        gain_side[r, 8:136, :] = spread(params_t[2, 8:136, :], r)
-        fade[r] = faded(params_t[0, 8:136, :], r)
+    @pl.loop(0, rows // 8)
+    def _(b):
+        turn = lax.rem(128 - 8 * b, 128)
+        for which in range(3):
+            table = pltpu.roll(params_t[which, 8:136, :], turn, 1)
+            for k in range(8):
+                r = 8 * b + k
+                wide = jnp.broadcast_to(table[:, k : k + 1], (128, 128))
+                if which == 0:
+                    nat[pl.ds(pl.multiple_of(r * 128, 128), 128), :] = (
+                        jnp.exp(wide * ages) * drain_cum[pl.ds(r, 1), :]
+                    )
+                elif kept == rows:
+                    (gain_self if which == 1 else gain_side)[r, 8:136, :] = wide
 
     rings[...] = jnp.zeros_like(rings)
 
@@ -144,48 +156,8 @@
     carry_t[8:136, :] = turned(carry)
     carry_t[136:144, :] = carry_e
 
-    def smooth(p, j):
-        above, here, below = (
-            lax.rem(jnp.maximum(j - 1, 0), RING),
-            lax.rem(j, RING),
-            lax.rem(jnp.minimum(j + 1, rows - 1), RING),
-        )
-        around = (
-            rings[p - 1, here, 9:153, :] + rings[p - 1, here, 7:151, :]
-            + rings[p - 1, above, 8:152, :] + rings[p - 1, below, 8:152, :]
-        )
-        return gain_self[j] * rings[p - 1, here, 8:152, :] + gain_side[j] * around
-
-    @pl.loop(0, rows + 4)
-    def _(i):
-        @pl.when(i < rows)
-        def _():
-            slot = lax.rem(i, RING)
-            odd = lax.rem(i, 2) == 1
-            enter = spread(carry_t[...], i)
-            rings[0, slot, 16:144, :] = local[i] + fade[i] * enter[8:136]
-            low, high = halo_in[0, i // 2], halo_in[1, i // 2]
-            low = jnp.where(odd, low, pltpu.roll(low, 4, 0))
-            high = jnp.where(odd, pltpu.roll(high, 4, 0), high)
-            rings[0, slot, 8:16, :] = low + faded(params_t[0, 0:8, :], i) * enter[0:8]
-            rings[0, slot, 144:152, :] = high + faded(params_t[0, 136:144, :], i) * enter[136:144]
-            gain_self[i, 0:8, :] = spread(params_t[1, 0:8, :], i)
-            gain_self[i, 136:144, :] = spread(params_t[1, 136:144, :], i)
-            gain_side[i, 0:8, :] = spread(params_t[2, 0:8, :], i)
-            gain_side[i, 136:144, :] = spread(params_t[2, 136:144, :], i)
-
-        for p in range(1, 5):
-            j = i - p
-
-            @pl.when(jnp.logical_and(j >= 0, j < rows))
-            def _():
-                new = smooth(p, j)
-                if p < 4:
-                    rings[p, lax.rem(j, RING), 8:152, :] = new
-                else:
-                    blocks[j] = new[8:136].astype(jnp.bfloat16)
-
     spot = gathered.at[me_l, :, pl.ds(pl.multiple_of(me_d * days, days), days)]
+    mine = pltpu.make_async_copy(blocks.at[me], spot, own_sem)
 
     def row_copy(k):
         other = lax.rem(me + k, count)
@@ -194,23 +166,112 @@
             (other // nl, lax.rem(other, nl)),
         )
 
+    back = me_l < nl // 2
+
+    def row(i):
+        return jnp.where(back, rows - 1 - i, i)
+
+    first = jnp.where(back, rows - nl * (me_d + 1), nl * me_d)
+
+    def smooth(p, i, low, high):
+        above, here, below = (
+            lax.rem(jnp.maximum(i - 1, low), RING),
+            lax.rem(i, RING),
+            lax.rem(jnp.minimum(i + 1, high - 1), RING),
+        )
+        gain = lax.rem(row(i), kept)
+        around = (
+            rings[p - 1, here, 9:153, :] + rings[p - 1, here, 7:151, :]
+            + rings[p - 1, above, 8:152, :] + rings[p - 1, below, 8:152, :]
+        )
+        return gain_self[gain] * rings[p - 1, here, 8:152, :] + gain_side[gain] * around
+
+    def enter_row(i):
+        r = row(i)
+        slot, gain = lax.rem(i, RING), lax.rem(r, kept)
+        odd = lax.rem(r, 2) == 1
+        enter = spread(carry_t[...], r)
+        fade = nat[pl.ds(pl.multiple_of(r * 128, 128), 128), :]
+        rings[0, slot, 16:144, :] = local[r] + fade * enter[8:136]
+        low, high = halo_in[0, r // 2], halo_in[1, r // 2]
+        low = jnp.where(odd, low, pltpu.roll(low, 4, 0))
+        high = jnp.where(odd, pltpu.roll(high, 4, 0), high)
+        rings[0, slot, 8:16, :] = low + faded(params_t[0, 0:8, :], r) * enter[0:8]
+        rings[0, slot, 144:152, :] = high + faded(params_t[0, 136:144, :], r) * enter[136:144]
+        if kept == rows:
+            parts = (slice(0, 8), slice(136, 144))
+        else:
+            parts = (slice(0, 144),)
+        for part in parts:
+            gain_self[gain, part, :] = spread(params_t[1, part, :], r)
+            gain_side[gain, part, :] = spread(params_t[2, part, :], r)
+
+    @pl.loop(0, 2)
+    def _(segment):
+        begin = segment == 0
+        low = jnp.where(begin, jnp.maximum(first - 4, 0), 0)
+        high = jnp.where(begin, rows, jnp.where(first == 0, 0, jnp.minimum(first + 4, rows)))
+        from_row = jnp.where(begin, first, 0)
+        to_row = jnp.where(begin, rows, first)
+
+        @pl.loop(low, jnp.where(high > low, high + 4, low))
+        def _(i):
+            @pl.when(i < high)
+            def _():
+                enter_row(i)
+
+            for p in range(1, 5):
+                j = i - p
+
+                if p < 4:
+                    @pl.when(jnp.logical_and(j >= low, j < high))
+                    def _():
+                        rings[p, lax.rem(j, RING), 8:152, :] = smooth(p, j, low, high)
+                else:
+                    @pl.when(jnp.logical_and(j >= from_row, j < to_row))
+                    def _():
+                        r = row(j)
+                        blocks[r] = smooth(p, j, low, high)[8:136].astype(jnp.bfloat16)
+
+                        @pl.when(r == me)
+                        def _():
+                            mine.start()
+
+                        @pl.when(r != me)
+                        def _():
+                            row_copy(lax.rem(r - me + count, count)).start()
+
+    fetch.wait()
+    mine.wait()
+
+    def result_copy(tile):
+        part = pl.ds(pl.multiple_of(tile * cells, cells), cells)
+        return pltpu.make_async_copy(result.at[:, part], out.at[:, part], out_sem.at[tile])
+
+    @pl.loop(0, nl)
+    def _(m):
+        tile = lax.rem(me_l + m, nl)
+        for d in range(nd):
+            k = lax.rem(me - d * nl - tile + count, count)
+
+            @pl.when(k > 0)
+            def _():
+                row_copy(k).wait_recv()
+
+        zone = zones[0, tile]
+        result[:, pl.ds(pl.multiple_of(tile * cells, cells), cells)] = lax.dot_general(
+            kernels_in[zone], gathered[tile], (((1,), (1,)), ((), ())),
+            preferred_element_type=F32,
+        ).astype(result.dtype)
+        result_copy(tile).start()
+
     @pl.loop(1, count)
     def _(k):
-        row_copy(k).start()
-
-    mine = pltpu.make_async_copy(blocks.at[me], spot, own_sem)
-    mine.start()
-    mine.wait()
-
-    @pl.loop(1, count)
-    def _(k):
-        row_copy(k).wait()
-
-
-def zone_kernel(zone_ids, kernel, block, out):
-    out[...] = lax.dot_general(
-        kernel[0], block[0], (((1,), (1,)), ((), ())), preferred_element_type=F32
-    ).astype(out.dtype)
+        row_copy(k).wait_send()
+
+    @pl.loop(0, nl)
+    def _(tile):
+        result_copy(tile).wait()
 
 
 def body(nd, nl, observed, decay_rate, drain_factor, smoothing, land_mask, zone_ids, kernels):
@@ -220,13 +281,14 @@
     assert days == 128 and cells == 128 and rows == count
     vmem = pl.BlockSpec(memory_space=pltpu.VMEM)
     dma = pltpu.SemaphoreType.DMA
-    gathered = pl.pallas_call(
+    kept = rows if rows <= 32 else 8
+    out = pl.pallas_call(
         functools.partial(series_kernel, nd, nl),
-        out_shape=jax.ShapeDtypeStruct((nl, cells, total), jnp.bfloat16),
-        in_specs=[vmem] * 5,
+        out_shape=jax.ShapeDtypeStruct((total, nl * cells), jnp.bfloat16),
+        in_specs=[pl.BlockSpec(memory_space=pltpu.SMEM)] + [vmem] * 5
+        + [pl.BlockSpec(memory_space=pl.ANY)],
         out_specs=pl.BlockSpec(memory_space=pl.ANY),
         scratch_shapes=[
-            pltpu.VMEM((rows, days), F32),
             pltpu.VMEM((rows, days), F32),
             pltpu.VMEM((days * rows, cells), F32),
             pltpu.VMEM((rows, cells, days), F32),
@@ -237,39 +299,26 @@
             pltpu.VMEM((3, 144, 128), F32),
             pltpu.VMEM((2, rows // 2, 8, days), F32),
             pltpu.VMEM((2, rows // 2, 8, days), F32),
-            pltpu.VMEM((rows, 144, 128), F32),
-            pltpu.VMEM((rows, 144, 128), F32),
-            pltpu.VMEM((rows, 128, 128), F32),
+            pltpu.VMEM((kept, 144, 128), F32),
+            pltpu.VMEM((kept, 144, 128), F32),
             pltpu.VMEM((144, 128), F32),
             pltpu.VMEM((4, RING, 160, 128), F32),
             pltpu.VMEM((rows, cells, days), jnp.bfloat16),
+            pltpu.VMEM(kernels.shape, jnp.bfloat16),
+            pltpu.VMEM((nl, cells, total), jnp.bfloat16),
+            pltpu.VMEM((total, nl * cells), jnp.bfloat16),
             dma((nd,)), dma((nd,)),
             dma((2, nd)), dma((2, nd)),
             dma((2,)), dma((2,)),
             dma((2,)), dma((2,)),
             dma((count,)), dma((count,)),
-            dma,
+            dma, dma, dma((nl,)),
         ],
         compiler_params=pltpu.CompilerParams(
-            collective_id=0, has_side_effects=True, vmem_limit_bytes=60 * 2**20
+            collective_id=0, has_side_effects=True, vmem_limit_bytes=62 * 2**20
         ),
         name="series",
-    )(observed, decay_rate, drain_factor, smoothing, land_mask)
-    out = pl.pallas_call(
-        zone_kernel,
-        out_shape=jax.ShapeDtypeStruct((total, nl * cells), jnp.bfloat16),
-        grid_spec=pltpu.PrefetchScalarGridSpec(
-            num_scalar_prefetch=1,
-            grid=(nl,),
-            in_specs=[
-                pl.BlockSpec((1, total, total), lambda k, zones: (zones[0, k], 0, 0)),
-                pl.BlockSpec((1, cells, total), lambda k, zones: (k, 0, 0)),
-            ],
-            out_specs=pl.BlockSpec((total, cells), lambda k, zones: (0, k)),
-        ),
-        compiler_params=pltpu.CompilerParams(vmem_limit_bytes=32 * 2**20),
-        name="zones",
-    )(zone_ids, kernels, gathered)
+    )(zone_ids, observed, decay_rate, drain_factor.T, smoothing, land_mask, kernels)
     return out.reshape(total, 1, nl * cells)
 
 

time: 63.9 us -> 47.4 us (0.74)
  Pallas kernels: 58.1 us -> 44.6 us
  local copies, waits for them, and re-layouts: 5.51 us -> 2.26 us
    pallas_call x1, Pallas kernels: 53.5 us -> 44.6 us  [body(): pl.pallas_call(functools.partial(series_kernel, nd, nl), out_shape=jax.Sh...]
    pallas_call x1 -> x0, Pallas kernels: 4.67 us -> none  [body(): pl.pallas_call(zone_kernel, out_shape=jax.ShapeDtypeStruct((total, nl * c...]
    unnamed x7 -> x1, local copies, waits for them, and re-layouts: 5.51 us -> 2.26 us
where the time goes in v1:
time: 47.4 us; the launch traced here: 46.8 us
  Pallas kernels  44.6 us (94%)
  local copies, waits for them, and re-layouts  2.26 us (5%)
    pallas_call x1, Pallas kernels, body(): pl.pallas_call(functools.partial(series_kernel, nd, nl), out_shape=jax.Sh...  44.6 us
    unnamed x1, local copies, waits for them, and re-layouts  2.26 us

profile of v1, /device:TPU:0, one launch (start us, length us, event | category | flops | bytes accessed | tf_op | source)
XLA Modules:
  0.0 46.8 jit_solution(573709570906053390)
XLA Ops:
  0.0 44.6 %series.1 = bf16[512,1024]{1,0:T(8,128)(2,1)} custom-call(s32[1,8]{1,0:T(1,128)} %zones.1, bf16[128,32,128]{2,1,0:T(8,128)(2,1)} %obs.1, f32[32,128]{1,0:T(8,128)} %decay.1, f32[32,128]{1,0:T(8,128)} %bitcast.3, f32[32,128]{1,0:T(8,128)} %smoothing.1, s32[32,128]{1,0:T(8,128)} %land.1, bf16[8,512,512]{2,1,0:T(8,128)(2,1)} %kernels.1), custom_call_target="tpu_custom_call" | custom-call | tf_op jit(solution)/shard_map/series/pallas_call | solution.py:285
  44.6 2.3 %copy.9 = bf16[512,1,1024]{2,0,1:T(8,128)(2,1)} copy(bf16[512,1,1024]{2,0,1:T(8,128)(2,1)} %bitcast.2) | data formatting | bytes 2097152

commit v2 on v1

--- a/solution.py
+++ b/solution.py
@@ -10,6 +10,7 @@
 MESH = pl.DeviceIdType.MESH
 F32 = jnp.float32
 RING = 4
+WIDE = 24 * 8
 
 
 def remote(src, dst, send, recv, device):
@@ -23,7 +24,7 @@
     nd, nl,
     zones, obs, decay, drain, smoothing, land, kernels, out,
     drain_cum, nat, local, summary, summary_in, summary_t, strip_in,
-    params_t, halo_out, halo_in, gain_self, gain_side, carry_t, rings, blocks,
+    params_t, halo_out, halo_in, weave, plain, gain_self, gain_side, carry_t, rings, blocks,
     kernels_in, gathered, result,
     sum_send, sum_recv, strip_send, strip_recv, par_send, par_recv,
     halo_send, halo_recv, row_send, row_recv, own_sem, kernels_sem, out_sem,
@@ -94,17 +95,19 @@
         copies.append(remote(summary, summary_in.at[k], sum_send.at[k], sum_recv.at[k], (there, me_l)))
         copies.append(remote(summary_t.at[:, 120:128, :], strip_in.at[0, k], strip_send.at[0, k], strip_recv.at[0, k], (there, east)))
         copies.append(remote(summary_t.at[:, 0:8, :], strip_in.at[1, k], strip_send.at[1, k], strip_recv.at[1, k], (there, west)))
-    copies.append(remote(params_t.at[:, 128:136, :], params_t.at[:, 0:8, :], par_send.at[0], par_recv.at[0], (me_d, east)))
-    copies.append(remote(params_t.at[:, 8:16, :], params_t.at[:, 136:144, :], par_send.at[1], par_recv.at[1], (me_d, west)))
-    for copy in copies:
+    params_copies = [
+        remote(params_t.at[:, 128:136, :], params_t.at[:, 0:8, :], par_send.at[0], par_recv.at[0], (me_d, east)),
+        remote(params_t.at[:, 8:16, :], params_t.at[:, 136:144, :], par_send.at[1], par_recv.at[1], (me_d, west)),
+    ]
+    for copy in params_copies + copies:
         copy.start()
 
     @pl.loop(0, rows // 2)
     def _(i):
         first = nat[pl.ds(2 * i, days, stride=rows), :].T
         second = nat[pl.ds(2 * i + 1, days, stride=rows), :].T
-        local[2 * i] = first
-        local[2 * i + 1] = second
+        local[2 * i, 8:136, :] = first
+        local[2 * i + 1, 8:136, :] = second
         halo_out[0, i] = jnp.concatenate([first[124:128], second[124:128]], axis=0)
         halo_out[1, i] = jnp.concatenate([first[0:4], second[0:4]], axis=0)
 
@@ -113,33 +116,32 @@
     copies[-2].start()
     copies[-1].start()
 
-    def column(table, r):
-        return pltpu.roll(table, lax.rem(128 - r, 128), 1)[:, 0:1]
-
-    def spread(table, r):
-        return jnp.broadcast_to(column(table, r), (table.shape[0], 128))
+    for copy in params_copies:
+        copy.wait()
+
+    def woven(rows_144):
+        return jnp.concatenate([rows_144[pl.ds(4 + j, 8, stride=16), :] for j in range(24)], axis=0)
+
+    for which in range(3):
+        weave[which] = woven(params_t.at[which])
+
+    def spread(table, k):
+        return jnp.broadcast_to(table[:, k : k + 1], (WIDE, 128))
+
+    def turn(b):
+        return lax.rem(128 - b, 128)
 
     ages = -(lax.broadcasted_iota(jnp.int32, (1, 128), 1) + 1).astype(F32)
 
-    def faded(table, r):
-        return jnp.exp(spread(table, r) * ages) * drain_cum[pl.ds(r, 1), :]
+    def full(r):
+        return pl.ds(pl.multiple_of(r * WIDE, WIDE), WIDE)
 
     @pl.loop(0, rows // 8)
     def _(b):
-        turn = lax.rem(128 - 8 * b, 128)
-        for which in range(3):
-            table = pltpu.roll(params_t[which, 8:136, :], turn, 1)
-            for k in range(8):
-                r = 8 * b + k
-                wide = jnp.broadcast_to(table[:, k : k + 1], (128, 128))
-                if which == 0:
-                    nat[pl.ds(pl.multiple_of(r * 128, 128), 128), :] = (
-                        jnp.exp(wide * ages) * drain_cum[pl.ds(r, 1), :]
-                    )
-                elif kept == rows:
-                    (gain_self if which == 1 else gain_side)[r, 8:136, :] = wide
-
-    rings[...] = jnp.zeros_like(rings)
+        table = pltpu.roll(weave[0], turn(8 * b), 1)
+        for k in range(8):
+            r = 8 * b + k
+            nat[full(r), :] = jnp.exp(spread(table, k) * ages) * drain_cum[pl.ds(r, 1), :]
 
     for copy in copies:
         copy.wait()
@@ -155,6 +157,24 @@
     carry_t[0:8, :] = carry_w
     carry_t[8:136, :] = turned(carry)
     carry_t[136:144, :] = carry_e
+    weave[0] = woven(carry_t)
+
+    def enter_rows(b):
+        table = pltpu.roll(weave[0], turn(8 * b), 1)
+        for k in range(8):
+            r = 8 * b + k
+            low, high = halo_in[0, 4 * b + k // 2], halo_in[1, 4 * b + k // 2]
+            if k % 2 == 0:
+                low = pltpu.roll(low, 4, 0)
+            else:
+                high = pltpu.roll(high, 4, 0)
+            local[r, 0:8, :] = low
+            local[r, 136:144, :] = high
+            nat[full(r), :] = woven(local.at[r]) + nat[full(r), :] * spread(table, k)
+        for which, gains in ((1, gain_self), (2, gain_side)):
+            table = pltpu.roll(weave[which], turn(8 * b), 1)
+            for k in range(8):
+                gains[lax.rem(8 * b + k, kept)] = spread(table, k)
 
     spot = gathered.at[me_l, :, pl.ds(pl.multiple_of(me_d * days, days), days)]
     mine = pltpu.make_async_copy(blocks.at[me], spot, own_sem)
@@ -171,75 +191,50 @@
     def row(i):
         return jnp.where(back, rows - 1 - i, i)
 
-    first = jnp.where(back, rows - nl * (me_d + 1), nl * me_d)
-
     def smooth(p, i, low, high):
-        above, here, below = (
-            lax.rem(jnp.maximum(i - 1, low), RING),
-            lax.rem(i, RING),
-            lax.rem(jnp.minimum(i + 1, high - 1), RING),
+        north, south = jnp.maximum(i - 1, low), jnp.minimum(i + 1, high - 1)
+        inner = pl.ds(8 * p, WIDE - 16 * p)
+
+        def line(j, start, size):
+            if p == 1:
+                return nat[pl.ds(pl.multiple_of(row(j) * WIDE + start, 8), size), :]
+            return rings[p - 2, lax.rem(j, RING), pl.ds(start, size), :]
+
+        gain = lax.rem(row(i), kept)
+        size = WIDE - 16 * p
+        here = line(i, 8 * p - 8, size + 16)
+        around = (
+            here[16:] + here[:-16] + line(north, 8 * p, size) + line(south, 8 * p, size)
         )
-        gain = lax.rem(row(i), kept)
-        around = (
-            rings[p - 1, here, 9:153, :] + rings[p - 1, here, 7:151, :]
-            + rings[p - 1, above, 8:152, :] + rings[p - 1, below, 8:152, :]
-        )
-        return gain_self[gain] * rings[p - 1, here, 8:152, :] + gain_side[gain] * around
-
-    def enter_row(i):
-        r = row(i)
-        slot, gain = lax.rem(i, RING), lax.rem(r, kept)
-        odd = lax.rem(r, 2) == 1
-        enter = spread(carry_t[...], r)
-        fade = nat[pl.ds(pl.multiple_of(r * 128, 128), 128), :]
-        rings[0, slot, 16:144, :] = local[r] + fade * enter[8:136]
-        low, high = halo_in[0, r // 2], halo_in[1, r // 2]
-        low = jnp.where(odd, low, pltpu.roll(low, 4, 0))
-        high = jnp.where(odd, pltpu.roll(high, 4, 0), high)
-        rings[0, slot, 8:16, :] = low + faded(params_t[0, 0:8, :], r) * enter[0:8]
-        rings[0, slot, 144:152, :] = high + faded(params_t[0, 136:144, :], r) * enter[136:144]
-        if kept == rows:
-            parts = (slice(0, 8), slice(136, 144))
-        else:
-            parts = (slice(0, 144),)
-        for part in parts:
-            gain_self[gain, part, :] = spread(params_t[1, part, :], r)
-            gain_side[gain, part, :] = spread(params_t[2, part, :], r)
-
-    @pl.loop(0, 2)
-    def _(segment):
-        begin = segment == 0
-        low = jnp.where(begin, jnp.maximum(first - 4, 0), 0)
-        high = jnp.where(begin, rows, jnp.where(first == 0, 0, jnp.minimum(first + 4, rows)))
-        from_row = jnp.where(begin, first, 0)
-        to_row = jnp.where(begin, rows, first)
-
-        @pl.loop(low, jnp.where(high > low, high + 4, low))
-        def _(i):
-            @pl.when(i < high)
+        return gain_self[gain, inner, :] * here[8:-8] + gain_side[gain, inner, :] * around
+
+    @pl.loop(0, rows + 4)
+    def _(i):
+        @pl.when(jnp.logical_and(lax.rem(i, 8) == 0, i < rows))
+        def _():
+            enter_rows(row(i) // 8)
+
+        for p in range(1, 5):
+            j = i - p
+
+            @pl.when(jnp.logical_and(j >= 0, j < rows))
             def _():
-                enter_row(i)
-
-            for p in range(1, 5):
-                j = i - p
-
+                new = smooth(p, j, 0, rows)
                 if p < 4:
-                    @pl.when(jnp.logical_and(j >= low, j < high))
+                    rings[p - 1, lax.rem(j, RING), pl.ds(8 * p, WIDE - 16 * p), :] = new
+                else:
+                    r = row(j)
+                    for v in range(16):
+                        plain[pl.ds(v, 8, stride=16), :] = new[8 * v : 8 * v + 8]
+                    blocks[r] = plain[...].astype(jnp.bfloat16)
+
+                    @pl.when(r == me)
                     def _():
-                        rings[p, lax.rem(j, RING), 8:152, :] = smooth(p, j, low, high)
-                else:
-                    @pl.when(jnp.logical_and(j >= from_row, j < to_row))
+                        mine.start()
+
+                    @pl.when(r != me)
                     def _():
-                        r = row(j)
-                        blocks[r] = smooth(p, j, low, high)[8:136].astype(jnp.bfloat16)
-
-                        @pl.when(r == me)
-                        def _():
-                            mine.start()
-
-                        @pl.when(r != me)
-                        def _():
-                            row_copy(lax.rem(r - me + count, count)).start()
+                        row_copy(lax.rem(r - me + count, count)).start()
 
     fetch.wait()
     mine.wait()
@@ -281,7 +276,7 @@
     assert days == 128 and cells == 128 and rows == count
     vmem = pl.BlockSpec(memory_space=pltpu.VMEM)
     dma = pltpu.SemaphoreType.DMA
-    kept = rows if rows <= 32 else 8
+    kept = min(rows, 16)
     out = pl.pallas_call(
         functools.partial(series_kernel, nd, nl),
         out_shape=jax.ShapeDtypeStruct((total, nl * cells), jnp.bfloat16),
@@ -290,8 +285,8 @@
         out_specs=pl.BlockSpec(memory_space=pl.ANY),
         scratch_shapes=[
             pltpu.VMEM((rows, days), F32),
-            pltpu.VMEM((days * rows, cells), F32),
-            pltpu.VMEM((rows, cells, days), F32),
+            pltpu.VMEM((rows * WIDE, cells), F32),
+            pltpu.VMEM((rows, 144, days), F32),
             pltpu.VMEM((2, rows, cells), F32),
             pltpu.VMEM((nd, 2, rows, cells), F32),
             pltpu.VMEM((2, cells, 128), F32),
@@ -299,10 +294,12 @@
             pltpu.VMEM((3, 144, 128), F32),
             pltpu.VMEM((2, rows // 2, 8, days), F32),
             pltpu.VMEM((2, rows // 2, 8, days), F32),
-            pltpu.VMEM((kept, 144, 128), F32),
-            pltpu.VMEM((kept, 144, 128), F32),
+            pltpu.VMEM((3, WIDE, 128), F32),
+            pltpu.VMEM((128, 128), F32),
+            pltpu.VMEM((kept, WIDE, 128), F32),
+            pltpu.VMEM((kept, WIDE, 128), F32),
             pltpu.VMEM((144, 128), F32),
-            pltpu.VMEM((4, RING, 160, 128), F32),
+            pltpu.VMEM((3, RING, WIDE, 128), F32),
             pltpu.VMEM((rows, cells, days), jnp.bfloat16),
             pltpu.VMEM(kernels.shape, jnp.bfloat16),
             pltpu.VMEM((nl, cells, total), jnp.bfloat16),

time: 47.4 us -> 44.9 us (0.947)
  the two profiles are of different devices: /device:TPU:0 before, /device:TPU:15 now
where the time goes in v2:
time: 44.9 us; the launch traced here: 44.8 us
  Pallas kernels  42.5 us (95%)
  local copies, waits for them, and re-layouts  2.26 us (5%)
    pallas_call x1, Pallas kernels, body(): pl.pallas_call(functools.partial(series_kernel, nd, nl), out_shape=jax.Sh...  42.5 us
    unnamed x1, local copies, waits for them, and re-layouts  2.26 us

profile of v2, /device:TPU:15, one launch (start us, length us, event | category | flops | bytes accessed | tf_op | source)
XLA Modules:
  0.0 44.8 jit_solution(3417705862166190592)
XLA Ops:
  0.0 42.5 %series.1 = bf16[512,1024]{1,0:T(8,128)(2,1)} custom-call(s32[1,8]{1,0:T(1,128)} %zones.1, bf16[128,32,128]{2,1,0:T(8,128)(2,1)} %obs.1, f32[32,128]{1,0:T(8,128)} %decay.1, f32[32,128]{1,0:T(8,128)} %bitcast.3, f32[32,128]{1,0:T(8,128)} %smoothing.1, s32[32,128]{1,0:T(8,128)} %land.1, bf16[8,512,512]{2,1,0:T(8,128)(2,1)} %kernels.1), custom_call_target="tpu_custom_call" | custom-call | tf_op jit(solution)/shard_map/series/pallas_call | solution.py:280
  42.5 2.3 %copy.9 = bf16[512,1,1024]{2,0,1:T(8,128)(2,1)} copy(bf16[512,1,1024]{2,0,1:T(8,128)(2,1)} %bitcast.2) | data formatting | bytes 2097152
